TPU v7x, 128 devices: a whole 4x4x4 slice. The times are simulated.
128 devices in a mesh: dp: 64 (over y, x, z_lo, core), mp: 2 (over z_hi).
Axes of the slice: x: 4, y: 4, z: 4 (z_hi: 2, z_lo: 2; z = z_hi * 2 + z_lo), core: 2. Of those that a mesh axis runs over, the one named last changes fastest.
Arguments:
- views: bfloat16 [8192, 1024], P('dp', 'mp'), may hold values from -6 to 6
- view_study: int32 [8192], P('dp'), may hold values from -1 to 1023, as said below
- pool_query: bfloat16 [1024], P('mp'), may hold values from -0.1875 to 0.1875
- texts: bfloat16 [1024, 1024], P('dp', 'mp'), may hold values from -6 to 6
- logit_scale: float32 [1], replicated, may hold values from 20 to 100
- logit_bias: float32 [1], replicated, may hold values from -4 to -1
Outputs:
- grad_pooled: bfloat16 [1024, 1024], P('dp', 'mp')
- grad_text: bfloat16 [1024, 1024], P('dp', 'mp')
Inputs may be any that keep to these rules, and one draw needn't show every extreme that they name: `view_study`: study s is owned by dp index s // 16. Every study has 1 to 6 views, and some study has exactly 6. The slots of one dp index hold at most 2 views of one owner's studies, a bound reached in every draw; the views of one owner are spread over the dp indices as evenly as their number allows, and one owner holds at most 96 views, reached in every draw.
All inputs are finite; a program needn't handle non-finite values.
Results may differ from a plain program's by a relative error of at most 0.015.
Values may be sent and summed in bfloat16 or wider, within the bound.
A program may use at most 64 MiB of HBM per device.

v0:
```python
import jax
import jax.numpy as jnp
from jax import lax
from jax.sharding import PartitionSpec as P


def on_device(views, view_study, pool_query, texts, logit_scale, logit_bias):
    shards = lax.axis_size("dp")
    divide_into_pair = lax.axis_size("mp")
    stu_rows = texts.shape[0]
    slots = views.shape[0]
    capacity = slots // shards
    partial_scores = jnp.dot(views, pool_query, preferred_element_type=jnp.float32)
    scores = lax.psum(partial_scores, "mp")
    weights = jax.nn.sigmoid(scores).astype(jnp.bfloat16)
    valid = view_study >= 0
    owner = jnp.where(valid, view_study // stu_rows, shards)
    owner_hot = (owner[:, None] == jnp.arange(shards)[None, :]).astype(jnp.int32)
    earlier = jnp.cumsum(owner_hot, axis=0) - owner_hot
    position = jnp.sum(earlier * owner_hot, axis=1)
    target_labels = jnp.where(valid, owner * capacity + position, slots)
    send_views = jnp.zeros_like(views).at[target_labels].set(views, mode="drop")
    send_weights = jnp.zeros((slots,), jnp.bfloat16).at[target_labels].set(weights, mode="drop")
    local_study = (view_study % stu_rows).astype(jnp.bfloat16)
    send_study = (
        jnp.full((slots,), -1.0, jnp.bfloat16).at[target_labels].set(local_study, mode="drop")
    )
    received = (
        lax.all_to_all(
            send_views.reshape(shards, capacity, -1), "dp", split_axis=0, concat_axis=0, tiled=True
        ),
        lax.all_to_all(
            send_weights.reshape(shards, capacity), "dp", split_axis=0, concat_axis=0, tiled=True
        ),
        lax.all_to_all(
            send_study.reshape(shards, capacity), "dp", split_axis=0, concat_axis=0, tiled=True
        ),
    )
    recv_views = received[0].reshape(slots, -1)
    recv_weights = received[1].reshape(slots)
    recv_study = received[2].reshape(slots)
    matches = (
        recv_study.astype(jnp.float32)[:, None] == jnp.arange(stu_rows, dtype=jnp.float32)[None, :]
    )
    pool_table = jnp.where(matches, recv_weights.astype(jnp.float32)[:, None], 0.0)
    numerator = jnp.einsum(
        "vs,vd->sd", pool_table.astype(jnp.bfloat16), recv_views, preferred_element_type=jnp.float32
    )
    denominator = jnp.sum(pool_table, axis=0)
    pooled = numerator / denominator[:, None]
    text_wide = texts.astype(jnp.float32)
    image_total, text_gradient_total = lax.psum(
        (jnp.sum(pooled * pooled, axis=1), jnp.sum(text_wide * text_wide, axis=1)), "mp"
    )
    study_emb = (pooled * lax.rsqrt(image_total + 1e-06)[:, None]).astype(jnp.bfloat16)
    report_emb = (text_wide * lax.rsqrt(text_gradient_total + 1e-06)[:, None]).astype(jnp.bfloat16)
    collected_narratives = lax.all_gather(report_emb, "dp", axis=0, tiled=True)
    collected_exam_vectors = collected_narratives.shape[0]
    scale_value = logit_scale[0]
    bias_value = logit_bias[0]
    dp_rank = lax.axis_index("dp")
    mp_rank = lax.axis_index("mp")
    shard_own_portion = collected_exam_vectors // divide_into_pair
    line_positions = collected_narratives
    summed = lax.psum_scatter(
        jnp.einsum(
            "jd,id->ji", line_positions, study_emb, preferred_element_type=jnp.float32
        ).astype(jnp.bfloat16),
        "mp",
        scatter_dimension=0,
        tiled=True,
    ).astype(jnp.float32)
    logits = scale_value * summed + bias_value
    report_ids = mp_rank * shard_own_portion + jnp.arange(shard_own_portion)
    study_ids = dp_rank * stu_rows + jnp.arange(stu_rows)
    diagonal = (report_ids[:, None] == study_ids[None, :]).astype(jnp.float32)
    slope = (jax.nn.sigmoid(logits) - diagonal).astype(jnp.bfloat16)
    collected_derivative_factor = lax.all_gather(slope, "mp", axis=0, tiled=True)
    grad_pooled = jnp.einsum(
        "js,jd->sd",
        collected_derivative_factor,
        collected_narratives,
        preferred_element_type=jnp.float32,
    ).astype(jnp.bfloat16)
    line_positions = collected_derivative_factor
    grad_text = lax.psum_scatter(
        jnp.dot(line_positions, study_emb, preferred_element_type=jnp.float32),
        "dp",
        scatter_dimension=0,
        tiled=True,
    )
    return (grad_pooled, grad_text.astype(jnp.bfloat16))


def solution(mesh):
    in_specs = (P("dp", "mp"), P("dp"), P("mp"), P("dp", "mp"), P(), P())
    out_specs = (P("dp", "mp"), P("dp", "mp"))
    return jax.shard_map(
        on_device, mesh=mesh, in_specs=in_specs, out_specs=out_specs, check_vma=False
    )
```

profile of v0, /device:TPU:1, one launch (start us, length us, event | category | flops | bytes accessed | tf_op | source)
XLA Modules:
  0.0 485.6 jit_solution(710534371898685818)
XLA Ops:
  7.2 0.7 fusion.8
  7.8 0.1 fusion.2
  7.9 0.2 reduce_window_sum.11
  8.1 0.2 select_reduce_fusion
  8.3 0.7 compare_select_fusion
  8.9 1.3 scatter_custom_fusion
  10.3 0.8 all_to_all.20
  11.1 10.3 %all-to-all-start = ((bf16[64,1,2]{2,1,0:T(2,128)(2,1)}), bf16[64,1,2]{2,1,0:T(2,128)(2,1)S(1)}, u32[]{:S(2)}, u32[]{:S(2)}) async-start(bf16[64,1,2]{2,1,0:T(2,128)(2,1)} %all_to_all.20), calls=%async_computation | async-start | bytes 65536 | tf_op jit(solution)/shard_map/all_to_all | solution.py:35
  21.4 0.8 fusion.3
  22.3 0.7 reshape.79
  22.9 1.0 convolution_bitcast_fusion
  24.0 5.6 %psum.22 = f32[128]{0:T(128)S(1)} all-reduce(f32[128]{0:T(128)S(1)} %convolution_bitcast_fusion), channel_id=1, replica_groups=mesh['dp'=64,'mp'=2] {'mp'}, use_global_device_ids=true, to_apply=%region_5.6 | all-reduce | flops 128 | bytes 1024 | tf_op jit(solution)/shard_map/psum | solution.py:14
  29.6 1.5 scatter_custom_fusion.2
  31.1 1.3 scatter_custom_fusion.1
  32.4 0.8 all_to_all.21
  33.2 0.7 reshape.48
  33.9 0.0 all-to-all-done
  33.9 9.7 %all-to-all-start.1 = ((bf16[64,1,2]{2,1,0:T(2,128)(2,1)}), bf16[64,1,2]{2,1,0:T(2,128)(2,1)S(1)}, u32[]{:S(2)}, u32[]{:S(2)}) async-start(bf16[64,1,2]{2,1,0:T(2,128)(2,1)} %all_to_all.21), calls=%async_computation.1 | async-start | bytes 65536 | tf_op jit(solution)/shard_map/all_to_all | solution.py:32
  43.6 0.1 convert_reduce_fusion.1
  43.7 7.6 %all-to-all-done.1 = bf16[64,1,2]{2,1,0:T(2,128)(2,1)S(1)} async-done(((bf16[64,1,2]{2,1,0:T(2,128)(2,1)}), bf16[64,1,2]{2,1,0:T(2,128)(2,1)S(1)}, u32[]{:S(2)}, u32[]{:S(2)}) %all-to-all-start.1) | async-done | bytes 288 | tf_op jit(solution)/shard_map/all_to_all | solution.py:32
  51.3 4.8 all-to-all-start.2
  56.1 0.0 all-gather.2.cloned.1.call-start
  56.2 0.1 convert_reduce_fusion
  56.3 0.1 reshape.50
  56.4 0.1 reshape.51
  56.5 0.1 select_reduce_fusion.1
  56.7 7.9 %all-to-all-done.2 = bf16[64,2,512]{2,1,0:T(2,128)(2,1)S(1)} async-done(((bf16[64,2,512]{2,1,0:T(2,128)(2,1)}), bf16[64,2,512]{2,1,0:T(2,128)(2,1)S(1)}, u32[]{:S(2)}, u32[]{:S(2)}) %all-to-all-start.2) | async-done | bytes 131104 | tf_op jit(solution)/shard_map/all_to_all | solution.py:29
  64.6 0.1 reshape.49
  64.7 0.2 multiply_reduce_fusion
  64.9 5.6 %all-reduce = (f32[16]{0:T(128)S(1)}, f32[16]{0:T(128)S(1)}) all-reduce(f32[16]{0:T(128)S(1)} %fusion.3, f32[16]{0:T(128)S(1)} %get-tuple-element.6), channel_id=1, replica_groups=mesh['dp'=64,'mp'=2] {'mp'}, use_global_device_ids=true, to_apply=%region_1.2 | all-reduce | flops 32 | bytes 256 | tf_op jit(solution)/shard_map/psum | solution.py:52
  70.5 1.4 fusion.4
  71.9 0.0 all-gather.2.cloned.1.call-update
  72.0 0.0 reduce-scatter.3.cloned.1.call-start
  73.3 99.6 %all-gather.2.cloned.1.call-done = bf16[1024,512]{1,0:T(8,128)(2,1)} async-done(((bf16[16,512]{1,0:T(8,128)(2,1)}), bf16[1024,512]{1,0:T(8,128)(2,1)}) %all-gather.2.cloned.1.call-update) | async-done | bytes 1048592 | tf_op jit(solution)/shard_map/all_gather | solution.py:57
  172.9 2.2 convolution_convert_fusion
  175.1 0.0 reduce-scatter.3.cloned.1.call-update
  175.2 0.0 reduce-scatter.5.cloned.1.call-start
  175.2 12.3 %reduce-scatter.3.cloned.1.call-done = bf16[512,16]{0,1:T(8,128)(2,1)} async-done(((bf16[1024,16]{0,1:T(8,128)(2,1)}), bf16[512,16]{0,1:T(8,128)(2,1)}) %reduce-scatter.3.cloned.1.call-update) | async-done | bytes 16400 | tf_op jit(solution)/shard_map/reduce_scatter | solution.py:65
  187.6 0.8 subtract_convert_fusion
  188.4 4.8 all_gather.7
  193.1 0.0 copy-start
  193.1 1.8 fusion.14
  195.0 0.0 reduce-scatter.5.cloned.1.call-update
  195.0 0.0 copy-done
  195.0 0.9 convolution_convert_fusion.1
  195.9 281.8 %reduce-scatter.5.cloned.1.call-done = f32[16,512]{1,0:T(8,128)} async-done(((f32[1024,512]{1,0:T(8,128)}), f32[16,512]{1,0:T(8,128)}) %reduce-scatter.5.cloned.1.call-update) | async-done | bytes 32784 | tf_op jit(solution)/shard_map/reduce_scatter | solution.py:86
  477.7 1.4 convert_element_type.75
  (5 shorter events, 0.0 us)
Async XLA Ops:
  11.1 22.8 %all-to-all-start = ((bf16[64,1,2]{2,1,0:T(2,128)(2,1)}), bf16[64,1,2]{2,1,0:T(2,128)(2,1)S(1)}, u32[]{:S(2)}, u32[]{:S(2)}) async-start(bf16[64,1,2]{2,1,0:T(2,128)(2,1)} %all_to_all.20), calls=%async_computation | async-start | bytes 65536 | tf_op jit(solution)/shard_map/all_to_all | solution.py:35
  33.9 17.4 %all-to-all-start.1 = ((bf16[64,1,2]{2,1,0:T(2,128)(2,1)}), bf16[64,1,2]{2,1,0:T(2,128)(2,1)S(1)}, u32[]{:S(2)}, u32[]{:S(2)}) async-start(bf16[64,1,2]{2,1,0:T(2,128)(2,1)} %all_to_all.21), calls=%async_computation.1 | async-start | bytes 65536 | tf_op jit(solution)/shard_map/all_to_all | solution.py:32
  51.3 13.3 %all-to-all-start.2 = ((bf16[64,2,512]{2,1,0:T(2,128)(2,1)}), bf16[64,2,512]{2,1,0:T(2,128)(2,1)S(1)}, u32[]{:S(2)}, u32[]{:S(2)}) async-start(bf16[64,2,512]{2,1,0:T(2,128)(2,1)} %reshape.48), calls=%async_computation.2 | async-start | bytes 262144 | tf_op jit(solution)/shard_map/all_to_all | solution.py:29
  56.1 116.8 %all-gather.2.cloned.1.call-start = ((), (), s32[]{:S(2)}) async-start(), calls=%async_computation.5 | async-start | bytes 1064960 | tf_op jit(solution)/shard_map/all_gather | solution.py:57
  72.0 115.6 %reduce-scatter.3.cloned.1.call-start = ((), (), s32[]{:S(2)}) async-start(), calls=%async_computation.6 | async-start | bytes 49152 | tf_op jit(solution)/shard_map/reduce_scatter | solution.py:65
  175.2 302.5 %reduce-scatter.5.cloned.1.call-start = ((), (), s32[]{:S(2)}) async-start(), calls=%async_computation.7 | async-start | bytes 2129920 | tf_op jit(solution)/shard_map/reduce_scatter | solution.py:86
  193.1 1.9 copy-start
Sparse Core Ops, SparseCore 0:
  72.1 100.8 all-gather.1
  175.3 12.2 reduce-scatter.2
  195.1 282.5 reduce-scatter.4
where the time goes:
time: 491 us; the launch traced here: 486 us
  waiting for transfers between devices  409 us (83%)
  starting transfers between devices  25 us (5%)
  blocking collectives  16 us (3%)
  between operations  15.2 us (3%)
  local copies, waits for them, and re-layouts  7.4 us (2%)
  other arithmetic  6.49 us (1%)
  matrix products  6.17 us (1%)
    reduce_scatter x1, waiting for transfers between devices, on_device(): lax.psum_scatter(jnp.dot(line_positions, study_emb, preferred_element_typ...  282 us
    all_gather x1, waiting for transfers between devices, on_device(): collected_narratives = lax.all_gather(report_emb, 'dp', axis=0, tiled=True)  99.6 us
    reduce_scatter x1, waiting for transfers between devices, on_device(): lax.psum_scatter(jnp.einsum('jd,id->ji', line_positions, study_emb, prefe...  12.3 us
    all_to_all x1, starting transfers between devices, on_device(): lax.all_to_all(send_study.reshape(shards, capacity), 'dp', split_axis=0,...  10.3 us
  transfers between devices with their start and end apart: 6, of which 5 were waited for; matrix products, arithmetic and copies ran while one was open for 2% of the time, Pallas kernels for 0%

commit v1 on v0

v1 whole, which is shorter than its diff:
```python
import jax
import jax.numpy as jnp
from jax import lax
from jax.experimental import pallas as pl
from jax.experimental.pallas import tpu as pltpu
from jax.sharding import PartitionSpec as P

MESH = pl.DeviceIdType.MESH
BF, F32 = jnp.bfloat16, jnp.float32
POS, LANES, HALVES = 16, 4, 2
OWN = 16
WIDTH = 512
SLOTS = 8
COL = LANES * OWN
BLK = 8
REP = BLK * OWN
CHUNK = 64
WIDE = WIDTH + 128


def nt(a, b):
    return lax.dot_general(a, b, (((1,), (1,)), ((), ())), preferred_element_type=F32)


def tn(a, b):
    return lax.dot_general(a, b, (((0,), (0,)), ((), ())), preferred_element_type=F32)


def kernel(
    views, study, query, texts, scale, bias, out_pooled, out_text,
    send_v, land_v, send_m, land_m, land_x, part, land_sib, col_sum, land_sum,
    text_part, pooled_part, land_t, land_p, ssem, rsem,
):
    dp, half = lax.axis_index("dp"), lax.axis_index("mp")
    pos, lane = dp // LANES, lax.rem(dp, LANES)
    zlo, core = lane // 2, lax.rem(lane, 2)
    other = 1 - half
    sel = lax.rem(pos, 2)
    selfish = sel == half

    barrier = pltpu.get_barrier_semaphore()

    def greet(p, l, h):
        pl.semaphore_signal(barrier, inc=1, device_id=(p * LANES + l, h), device_id_type=MESH)

    def greet_far(k, carry):
        greet(lax.rem(pos + k, POS), lane, other)
        return carry

    def greet_near(k, carry):
        greet(lax.rem(pos + k, POS), lane, half)
        return carry

    lax.fori_loop(0, POS, greet_far, 0)
    lax.fori_loop(1, POS, greet_near, 0)
    for k in range(1, LANES):
        for h in (half, other):
            greet(pos, lax.rem(lane + k, LANES), h)

    slots = views.shape[0]
    row = lax.broadcasted_iota(jnp.int32, (slots, slots), 0)
    colm = lax.broadcasted_iota(jnp.int32, (slots, slots), 1)
    ids = study[...]
    mine = (ids >> 4) == (row >> 1)
    before = (row < colm).astype(F32).astype(BF)
    hot = mine.astype(F32).astype(BF)
    rank = jnp.dot(hot, before, preferred_element_type=F32)
    pick = jnp.where(mine & (rank == (row & 1).astype(F32)), 1.0, 0.0).astype(BF)
    packed = jnp.dot(pick, views[...], preferred_element_type=F32)
    marks = jnp.broadcast_to(((ids & (COL - 1)) + 1).astype(F32), (slots, slots)).astype(BF)
    mark = nt(pick, marks)
    score = nt(packed.astype(BF), jnp.broadcast_to(query[...].astype(F32), (128, WIDTH)).astype(BF))
    high = score.astype(BF).astype(F32)
    mid = (score - high).astype(BF).astype(F32)
    low = score - high - mid
    parts = [packed[:, q * 128 : (q + 1) * 128] for q in range(4)] + [mark, high, mid, low]
    chunks = jnp.concatenate([x.reshape(POS, 1, SLOTS, 128) for x in parts], axis=1)
    send_v[...] = chunks.reshape(POS * CHUNK, 128).astype(BF)
    send_m[...] = score
    mine_rows = pl.ds(pl.multiple_of(pos * CHUNK, CHUNK), CHUNK)
    land_v[mine_rows] = send_v[mine_rows]

    pl.semaphore_wait(barrier, 2 * POS - 1 + 6)

    def copy(src, dst, i, p, l, h):
        return pltpu.make_async_remote_copy(
            src_ref=src, dst_ref=dst, send_sem=ssem.at[i], recv_sem=rsem.at[i],
            device_id=(p * LANES + l, h), device_id_type=MESH,
        )

    def done(ref, sem):
        pltpu.make_async_copy(ref, ref, sem).wait()

    def send_far(k, carry):
        p = lax.rem(pos + k, POS)
        copy(
            send_m.at[pl.ds(pl.multiple_of(p * SLOTS, SLOTS), SLOTS)],
            land_m.at[pl.ds(pl.multiple_of(pos * SLOTS, SLOTS), SLOTS)], 1, p, lane, other,
        ).start()
        return carry

    def send_near(k, carry):
        p = lax.rem(pos + k, POS)
        copy(
            send_v.at[pl.ds(pl.multiple_of(p * CHUNK, CHUNK), CHUNK)],
            land_v.at[mine_rows], 0, p, lane, half,
        ).start()
        return carry

    lax.fori_loop(0, POS, send_far, 0)
    lax.fori_loop(1, POS, send_near, 0)

    text_rows = pl.ds(pl.multiple_of((pos // 2) * OWN, OWN), OWN)

    def send_text(k, carry):
        p = lax.rem(pos + k, POS)
        copy(texts, land_x.at[half, text_rows], 2, p, lane, sel).start()
        return carry

    lax.fori_loop(1, POS, send_text, 0)

    @pl.when(selfish)
    def _():
        land_x[half, text_rows] = texts[...]

    @pl.when(jnp.logical_not(selfish))
    def _():
        copy(texts, land_x.at[half, text_rows], 2, pos, lane, sel).start()

    def done_but_self(ref, rows, sem):
        @pl.when(selfish)
        def _():
            done(ref.at[pl.ds(0, rows - OWN)], sem)

        @pl.when(jnp.logical_not(selfish))
        def _():
            done(ref, sem)

    done(land_m, rsem.at[1])
    done(land_v.at[pl.ds(0, (POS - 1) * CHUNK)], rsem.at[0])
    got = land_v[...].astype(F32).reshape(POS, 8, SLOTS, 128)
    got = [got[:, q].reshape(slots, 128) for q in range(8)]
    total = (got[5] + got[6] + got[7]) + land_m[...]
    weight = jax.nn.sigmoid(total).astype(BF).astype(F32)
    table = jnp.where(got[4] == (colm + 1).astype(F32), weight, 0.0).astype(BF)[:, :COL]
    wide = jnp.concatenate([x.astype(BF) for x in got[:4]] + [jnp.ones((slots, 128), BF)], axis=1)
    sums = tn(table, wide)
    part[...] = sums.astype(BF)
    sib = copy(part, land_sib, 3, pos, lane + 1 - 2 * core, half)
    sib.start()
    sib.wait_recv()
    col_sum[...] = (sums + land_sib[...].astype(F32)).astype(BF)
    z = half * 2 + zlo
    for k in range(1, 4):
        there = lax.rem(z + k, 4)
        copy(col_sum, land_sum.at[z], 4, pos, lax.rem(there, 2) * 2 + core, there // 2).start()
    land_sum[z] = col_sum[...]

    done_but_self(land_x.reshape(2 * REP, WIDTH), 2 * REP, rsem.at[2])
    raw = [land_x[0].astype(F32), land_x[1].astype(F32)]
    norm = jnp.sum(raw[0] * raw[0] + raw[1] * raw[1], axis=1, keepdims=True)
    inv = lax.rsqrt(norm + 1e-06)
    report = jnp.concatenate([(x * inv).astype(BF) for x in raw], axis=1)

    done(land_sum.at[pl.ds(0, 3)], rsem.at[4])
    both = [
        land_sum[2 * h].astype(F32) + land_sum[2 * h + 1].astype(F32) for h in range(HALVES)
    ]
    mean = [x[:, :WIDTH] / x[:, WIDTH : WIDTH + 1] for x in both]
    norm = jnp.sum(mean[0] * mean[0] + mean[1] * mean[1], axis=1, keepdims=True)
    inv = lax.rsqrt(norm + 1e-06)
    unit = jnp.concatenate([(x * inv).astype(BF) for x in mean], axis=1)

    logits = scale[0] * nt(unit, report) + bias[0]
    i = lax.broadcasted_iota(jnp.int32, (COL, REP), 0)
    j = lax.broadcasted_iota(jnp.int32, (COL, REP), 1)
    study_id = pos * COL + i
    report_id = ((2 * (j // OWN) + half) * LANES + lane) * OWN + lax.rem(j, OWN)
    own = (study_id == report_id).astype(F32)
    slope = (jax.nn.sigmoid(logits) - own).astype(BF)

    gt = tn(slope, unit).astype(BF)
    for h in range(HALVES):
        text_part[h] = gt[:, h * WIDTH : (h + 1) * WIDTH]

    def give_text(k, carry):
        b = lax.rem(pos // 2 + k // 2, BLK)
        h = lax.rem(half + k, 2)
        rows = pl.ds(pl.multiple_of(b * OWN, OWN), OWN)
        copy(text_part.at[h, rows], land_t.at[pos], 5, 2 * b + half, lane, h).start()
        return carry

    lax.fori_loop(1, 2 * BLK, give_text, 0)
    own_rows = pl.ds(pl.multiple_of((pos // 2) * OWN, OWN), OWN)

    @pl.when(selfish)
    def _():
        land_t[pos] = text_part[half, own_rows]

    @pl.when(jnp.logical_not(selfish))
    def _():
        b = pos // 2
        copy(text_part.at[half, own_rows], land_t.at[pos], 5, 2 * b + half, lane, half).start()

    gp = jnp.dot(slope, report, preferred_element_type=F32).astype(BF)
    for h in range(HALVES):
        pooled_part[h] = gp[:, h * WIDTH : (h + 1) * WIDTH]
    me = lane * 2 + half

    def give_pooled(k, carry):
        there = lax.rem(me + k, 8)
        l, h = there // 2, lax.rem(there, 2)
        rows = pl.ds(pl.multiple_of(l * OWN, OWN), OWN)
        copy(pooled_part.at[h, rows], land_p.at[me], 6, pos, l, h).start()
        return carry

    lax.fori_loop(1, 8, give_pooled, 0)
    land_p[me] = pooled_part[half, pl.ds(pl.multiple_of(lane * OWN, OWN), OWN)]

    done(land_p.at[pl.ds(0, 7)], rsem.at[6])
    out_pooled[...] = jnp.sum(land_p[...].astype(F32), axis=0).astype(BF)
    done_but_self(land_t.reshape(POS * OWN, WIDTH), POS * OWN, rsem.at[5])
    out_text[...] = jnp.sum(land_t[...].astype(F32), axis=0).astype(BF)

    done(send_v.at[pl.ds(0, (POS - 1) * CHUNK)], ssem.at[0])
    done(send_m, ssem.at[1])
    done_but_self(land_x.reshape(2 * REP, WIDTH), 2 * REP, ssem.at[2])
    sib.wait_send()
    done(land_sum.at[pl.ds(0, 3)], ssem.at[4])
    done_but_self(land_t.reshape(POS * OWN, WIDTH), POS * OWN, ssem.at[5])
    done(land_p.at[pl.ds(0, 7)], ssem.at[6])


def on_device(views, view_study, pool_query, texts, logit_scale, logit_bias):
    slots = views.shape[0]
    vmem = pl.BlockSpec(memory_space=pltpu.VMEM)
    smem = pl.BlockSpec(memory_space=pltpu.SMEM)
    out = jax.ShapeDtypeStruct((OWN, WIDTH), BF)
    return pl.pallas_call(
        kernel,
        out_shape=(out, out),
        in_specs=[vmem, vmem, vmem, vmem, smem, smem],
        out_specs=(vmem, vmem),
        scratch_shapes=[
            pltpu.VMEM((POS * CHUNK, 128), BF),
            pltpu.VMEM((POS * CHUNK, 128), BF),
            pltpu.VMEM((slots, 128), F32),
            pltpu.VMEM((slots, 128), F32),
            pltpu.VMEM((HALVES, REP, WIDTH), BF),
            pltpu.VMEM((COL, WIDE), BF),
            pltpu.VMEM((COL, WIDE), BF),
            pltpu.VMEM((COL, WIDE), BF),
            pltpu.VMEM((4, COL, WIDE), BF),
            pltpu.VMEM((HALVES, REP, WIDTH), BF),
            pltpu.VMEM((HALVES, COL, WIDTH), BF),
            pltpu.VMEM((POS, OWN, WIDTH), BF),
            pltpu.VMEM((LANES * HALVES, OWN, WIDTH), BF),
            pltpu.SemaphoreType.DMA((7,)),
            pltpu.SemaphoreType.DMA((7,)),
        ],
        compiler_params=pltpu.CompilerParams(
            collective_id=0, has_side_effects=True, vmem_limit_bytes=32 << 20
        ),
    )(
        views, view_study.reshape(1, slots), pool_query.reshape(1, WIDTH), texts,
        logit_scale, logit_bias,
    )


def solution(mesh):
    in_specs = (P("dp", "mp"), P("dp"), P("mp"), P("dp", "mp"), P(), P())
    out_specs = (P("dp", "mp"), P("dp", "mp"))
    return jax.shard_map(
        on_device, mesh=mesh, in_specs=in_specs, out_specs=out_specs, check_vma=False
    )
```

time: 491 us -> 39.7 us (0.08)
  the two profiles are of different devices: /device:TPU:1 before, /device:TPU:7 now
where the time goes in v1:
time: 39.7 us; the launch traced here: 39.5 us
  Pallas kernels  33.4 us (84%)
  local copies, waits for them, and re-layouts  4.16 us (10%)
  between operations  1.94 us (5%)
    pallas_call x1, Pallas kernels, on_device(): pl.pallas_call(kernel, out_shape=(out, out), in_specs=[vmem, vmem, vmem,...  33.4 us
    unnamed x10, local copies, waits for them, and re-layouts  4.16 us

profile of v1, /device:TPU:7, one launch (start us, length us, event | category | flops | bytes accessed | tf_op | source)
XLA Modules:
  0.0 39.5 jit_solution(6876545710078145923)
XLA Ops:
  1.9 0.0 copy-start.3
  1.9 0.7 %copy-done.3 = bf16[512]{0:T(512)(128)(2,1)S(1)} copy-done((bf16[512]{0:T(512)(128)(2,1)S(1)}, bf16[512]{0:T(512)(128)(2,1)}, u32[]{:S(2)}) %copy-start.3) | copy-done | bytes 1048
  2.6 0.0 copy-start.2
  2.6 0.6 %copy-done.2 = s32[128]{0:T(128)S(1)} copy-done((s32[128]{0:T(128)S(1)}, s32[128]{0:T(128)}, u32[]{:S(2)}) %copy-start.2) | copy-done | bytes 536
  3.3 0.0 copy-start
  3.3 0.9 %copy-done = bf16[128,512]{1,0:T(8,128)(2,1)S(1)} copy-done((bf16[128,512]{1,0:T(8,128)(2,1)S(1)}, bf16[128,512]{1,0:T(8,128)(2,1)}, u32[]{:S(2)}) %copy-start) | copy-done | bytes 131096
  4.2 0.0 copy-start.1
  4.2 0.7 %copy-done.1 = bf16[16,512]{1,0:T(8,128)(2,1)S(1)} copy-done((bf16[16,512]{1,0:T(8,128)(2,1)S(1)}, bf16[16,512]{1,0:T(8,128)(2,1)}, u32[]{:S(2)}) %copy-start.1) | copy-done | bytes 16408
  4.9 33.4 %shard_map.77 = (bf16[16,512]{1,0:T(8,128)(2,1)S(1)}, bf16[16,512]{1,0:T(8,128)(2,1)S(1)}) custom-call(bf16[128,512]{1,0:T(8,128)(2,1)S(1)} %copy-done, s32[1,128]{1,0:T(1,128)S(1)} %bitcast.1, bf16[1,512]{1,0:T(2,128)(2,1)S(1)} %reshape.11.query, bf16[16,512]{1,0:T(8,128)(2,1)S(1)} %copy-done.1, f32[1]{0:T(128)S(6)} %copy.10.scale, f32[1]{0:T(128)S(6)} %copy.11.bias), custom_call_target="tpu_custom_call" | custom-call | tf_op jit(solution)/shard_map/pallas_call | solution.py:239
  38.3 0.6 %copy.12 = bf16[16,512]{1,0:T(8,128)(2,1)} copy(bf16[16,512]{1,0:T(8,128)(2,1)S(1)} %get-tuple-element.4) | data formatting | bytes 32768
  38.9 0.6 %copy.13 = bf16[16,512]{1,0:T(8,128)(2,1)} copy(bf16[16,512]{1,0:T(8,128)(2,1)S(1)} %get-tuple-element.5) | data formatting | bytes 32768
  (1 shorter events, 0.0 us)
Async XLA Ops:
  1.9 0.7 %copy-start.3 = (bf16[512]{0:T(512)(128)(2,1)S(1)}, bf16[512]{0:T(512)(128)(2,1)}, u32[]{:S(2)}) copy-start(bf16[512]{0:T(512)(128)(2,1)} %param.8) | copy-start | bytes 3076
  2.6 0.7 %copy-start.2 = (s32[128]{0:T(128)S(1)}, s32[128]{0:T(128)}, u32[]{:S(2)}) copy-start(s32[128]{0:T(128)} %param.7) | copy-start | bytes 1540
  3.3 0.9 %copy-start = (bf16[128,512]{1,0:T(8,128)(2,1)S(1)}, bf16[128,512]{1,0:T(8,128)(2,1)}, u32[]{:S(2)}) copy-start(bf16[128,512]{1,0:T(8,128)(2,1)} %views.1) | copy-start | bytes 393220
  4.2 0.7 %copy-start.1 = (bf16[16,512]{1,0:T(8,128)(2,1)S(1)}, bf16[16,512]{1,0:T(8,128)(2,1)}, u32[]{:S(2)}) copy-start(bf16[16,512]{1,0:T(8,128)(2,1)} %texts.1) | copy-start | bytes 49156

commit v2 on v1

v2 whole, which is shorter than its diff:
```python
import jax
import jax.numpy as jnp
from jax import lax
from jax.experimental import pallas as pl
from jax.experimental.pallas import tpu as pltpu
from jax.sharding import PartitionSpec as P

MESH = pl.DeviceIdType.MESH
BF, F32 = jnp.bfloat16, jnp.float32
SIDE = 4
POS, LANES, HALVES = 16, 4, 2
OWN = 16
WIDTH = 512
SLOTS = 8
COL = LANES * OWN
BLK = 8
REP = BLK * OWN
CHUNK = 48
WIDE = WIDTH + 128

NEAR = {0: 0, 1: 1, 2: 2, 3: 1}
STEPS = sorted(
    ((dy, dx) for dy in range(SIDE) for dx in range(SIDE)), key=lambda s: -NEAR[s[0]] - NEAR[s[1]]
)


def nt(a, b):
    return lax.dot_general(a, b, (((1,), (1,)), ((), ())), preferred_element_type=F32)


def tn(a, b):
    return lax.dot_general(a, b, (((0,), (0,)), ((), ())), preferred_element_type=F32)


def kernel(
    views_in, study_in, query_in, texts_in, scale, bias, out_pooled, out_text,
    views, study, query, texts, send_v, land_v, send_s, land_s, land_x, part, land_sib, col_sum, land_sum,
    text_part, pooled_part, land_t, land_p, ssem, rsem, lsem,
):
    dp, half = lax.axis_index("dp"), lax.axis_index("mp")
    pos, lane = dp // LANES, lax.rem(dp, LANES)
    py, px = pos // SIDE, lax.rem(pos, SIDE)
    zlo, core = lane // 2, lax.rem(lane, 2)
    other = 1 - half
    cross = (1 - zlo) * 2 + core

    def at(dy, dx):
        return lax.rem(py + dy, SIDE) * SIDE + lax.rem(px + dx, SIDE)

    barrier = pltpu.get_barrier_semaphore()

    def greet(p, l, h):
        pl.semaphore_signal(barrier, inc=1, device_id=(p * LANES + l, h), device_id_type=MESH)

    for dy, dx in STEPS[:-1]:
        greet(at(dy, dx), lane, half)
    greet(pos, lane, other)
    for k in range(1, LANES):
        for h in (other, half):
            greet(pos, lax.rem(lane + k, LANES), h)

    loads = [
        pltpu.make_async_copy(a, b, lsem.at[i])
        for i, (a, b) in enumerate(
            [(study_in, study), (views_in, views), (query_in, query), (texts_in, texts)]
        )
    ]
    for load in loads:
        load.start()
    drains = []

    for load in loads:
        load.wait()

    slots = views.shape[0]
    row = lax.broadcasted_iota(jnp.int32, (slots, slots), 0)
    colm = lax.broadcasted_iota(jnp.int32, (slots, slots), 1)
    ids = study[...]
    mine = (ids >> 4) == (row >> 1)
    before = (row < colm).astype(F32).astype(BF)
    hot = mine.astype(F32).astype(BF)
    rank = jnp.dot(hot, before, preferred_element_type=F32)
    pick = jnp.where(mine & (rank == (row & 1).astype(F32)), 1.0, 0.0).astype(BF)
    packed = jnp.dot(pick, views[...], preferred_element_type=F32)
    marks = jnp.broadcast_to(((ids & (COL - 1)) + 1).astype(F32), (slots, slots)).astype(BF)
    mark = nt(pick, marks)
    parts = [packed[:, q * 128 : (q + 1) * 128] for q in range(4)] + [mark, mark]
    chunks = jnp.concatenate([x.reshape(POS, 1, SLOTS, 128) for x in parts], axis=1)
    send_v[...] = chunks.reshape(POS * CHUNK, 128).astype(BF)
    mine_rows = pl.ds(pl.multiple_of(pos * CHUNK, CHUNK), CHUNK)
    land_v[mine_rows] = send_v[mine_rows]
    ask = jnp.broadcast_to(query[...].reshape(1, WIDTH).astype(F32), (SLOTS, WIDTH)).astype(BF)

    pl.semaphore_wait(barrier, POS - 1 + 7)

    def copy(src, dst, i, p, l, h):
        return pltpu.make_async_remote_copy(
            src_ref=src, dst_ref=dst, send_sem=ssem.at[i], recv_sem=rsem.at[i],
            device_id=(p * LANES + l, h), device_id_type=MESH,
        )

    def done(ref, sem):
        pltpu.make_async_copy(ref, ref, sem).wait()

    for dy, dx in STEPS[:-1]:
        p = at(dy, dx)
        copy(
            send_v.at[pl.ds(pl.multiple_of(p * CHUNK, CHUNK), CHUNK)],
            land_v.at[mine_rows], 0, p, lane, half,
        ).start()
    drains.append(lambda: done(send_v.at[pl.ds(0, (POS - 1) * CHUNK)], ssem.at[0]))

    done(land_v.at[pl.ds(0, (POS - 1) * CHUNK)], rsem.at[0])
    got = land_v[...].astype(F32).reshape(POS, CHUNK // SLOTS, SLOTS, 128)
    got = [got[:, q].reshape(slots, 128).astype(BF) for q in range(5)]
    held = jnp.concatenate(got[:4], axis=1)
    score = nt(ask, held)
    send_s[...] = score
    swap = copy(send_s, land_s, 1, pos, lane, other)
    swap.start()
    drains.append(swap.wait_send)

    text_rows = pl.ds(pl.multiple_of((pos // 2) * OWN, OWN), OWN)
    sel = lax.rem(pos, 2)
    for dy, dx in STEPS:
        copy(texts, land_x.at[half, text_rows], 2, at(dy, dx), cross, sel).start()
    drains.append(lambda: done(land_x, ssem.at[2]))

    mark_row = nt(jnp.where(colm[:SLOTS] == 0, 1.0, 0.0).astype(BF), got[4])[:1]
    swap.wait_recv()
    weight = jax.nn.sigmoid(score + land_s[...]).astype(BF).astype(F32)[:1]
    table = jnp.where(mark_row == (row[:COL] + 1).astype(F32), weight, 0.0).astype(BF)
    wide = jnp.concatenate([held, jnp.ones((slots, 128), BF)], axis=1)
    sums = jnp.dot(table, wide, preferred_element_type=F32)
    part[...] = sums.astype(BF)
    sib = copy(part, land_sib, 3, pos, lane + 1 - 2 * core, half)
    sib.start()
    sib.wait_recv()
    drains.append(sib.wait_send)
    col_sum[...] = (sums + land_sib[...].astype(F32)).astype(BF)
    z = half * 2 + zlo
    for k in (2, 1, 3):
        there = lax.rem(z + k, 4)
        copy(col_sum, land_sum.at[z], 4, pos, lax.rem(there, 2) * 2 + core, there // 2).start()
    land_sum[z] = col_sum[...]
    drains.append(lambda: done(land_sum.at[pl.ds(0, 3)], ssem.at[4]))

    done(land_x, rsem.at[2])
    raw = [land_x[0].astype(F32), land_x[1].astype(F32)]
    norm = jnp.sum(raw[0] * raw[0] + raw[1] * raw[1], axis=1, keepdims=True)
    inv = lax.rsqrt(norm + 1e-06)
    report = jnp.concatenate([(x * inv).astype(BF) for x in raw], axis=1)

    done(land_sum.at[pl.ds(0, 3)], rsem.at[4])
    both = [
        land_sum[2 * h].astype(F32) + land_sum[2 * h + 1].astype(F32) for h in range(HALVES)
    ]
    mean = [x[:, :WIDTH] / x[:, WIDTH : WIDTH + 1] for x in both]
    norm = jnp.sum(mean[0] * mean[0] + mean[1] * mean[1], axis=1, keepdims=True)
    inv = lax.rsqrt(norm + 1e-06)
    unit = jnp.concatenate([(x * inv).astype(BF) for x in mean], axis=1)

    logits = scale[0] * nt(unit, report) + bias[0]
    i = lax.broadcasted_iota(jnp.int32, (COL, REP), 0)
    j = lax.broadcasted_iota(jnp.int32, (COL, REP), 1)
    study_id = pos * COL + i
    report_id = ((2 * (j // OWN) + half) * LANES + cross) * OWN + lax.rem(j, OWN)
    own = (study_id == report_id).astype(F32)
    slope = (jax.nn.sigmoid(logits) - own).astype(BF)

    gt = tn(slope, unit).astype(BF)
    for h in range(HALVES):
        text_part[h] = gt[:, h * WIDTH : (h + 1) * WIDTH]
    odd = lax.rem(px + half, 2)
    for dy in (2, 1, 3, 0):
        for dx in (2, 0):
            p = at(dy, dx + odd)
            rows = pl.ds(pl.multiple_of((p // 2) * OWN, OWN), OWN)
            for h in range(HALVES):
                copy(text_part.at[h, rows], land_t.at[pos], 5, p, cross, h).start()
    drains.append(lambda: done(land_t, ssem.at[5]))

    gp = jnp.dot(slope, report, preferred_element_type=F32).astype(BF)
    for h in range(HALVES):
        pooled_part[h] = gp[:, h * WIDTH : (h + 1) * WIDTH]
    me = lane * 2 + half
    for k in range(1, 8):
        there = lax.rem(me + k, 8)
        l, h = there // 2, lax.rem(there, 2)
        rows = pl.ds(pl.multiple_of(l * OWN, OWN), OWN)
        copy(pooled_part.at[h, rows], land_p.at[me], 6, pos, l, h).start()
    land_p[me] = pooled_part[half, pl.ds(pl.multiple_of(lane * OWN, OWN), OWN)]
    drains.append(lambda: done(land_p.at[pl.ds(0, 7)], ssem.at[6]))

    done(land_p.at[pl.ds(0, 7)], rsem.at[6])
    out_pooled[...] = jnp.sum(land_p[...].astype(F32), axis=0).astype(BF)
    done(land_t, rsem.at[5])
    out_text[...] = jnp.sum(land_t[...].astype(F32), axis=0).astype(BF)
    for drain in drains:
        drain()


def on_device(views, view_study, pool_query, texts, logit_scale, logit_bias):
    slots = views.shape[0]
    vmem = pl.BlockSpec(memory_space=pltpu.VMEM)
    hbm = pl.BlockSpec(memory_space=pltpu.HBM)
    smem = pl.BlockSpec(memory_space=pltpu.SMEM)
    out = jax.ShapeDtypeStruct((OWN, WIDTH), BF)
    return pl.pallas_call(
        kernel,
        out_shape=(out, out),
        in_specs=[hbm, hbm, hbm, hbm, smem, smem],
        out_specs=(vmem, vmem),
        scratch_shapes=[
            pltpu.VMEM((slots, WIDTH), BF),
            pltpu.VMEM((1, slots), jnp.int32),
            pltpu.VMEM((WIDTH,), BF),
            pltpu.VMEM((OWN, WIDTH), BF),
            pltpu.VMEM((POS * CHUNK, 128), BF),
            pltpu.VMEM((POS * CHUNK, 128), BF),
            pltpu.VMEM((SLOTS, 128), F32),
            pltpu.VMEM((SLOTS, 128), F32),
            pltpu.VMEM((HALVES, REP, WIDTH), BF),
            pltpu.VMEM((COL, WIDE), BF),
            pltpu.VMEM((COL, WIDE), BF),
            pltpu.VMEM((COL, WIDE), BF),
            pltpu.VMEM((4, COL, WIDE), BF),
            pltpu.VMEM((HALVES, REP, WIDTH), BF),
            pltpu.VMEM((HALVES, COL, WIDTH), BF),
            pltpu.VMEM((POS, OWN, WIDTH), BF),
            pltpu.VMEM((LANES * HALVES, OWN, WIDTH), BF),
            pltpu.SemaphoreType.DMA((7,)),
            pltpu.SemaphoreType.DMA((7,)),
            pltpu.SemaphoreType.DMA((4,)),
        ],
        compiler_params=pltpu.CompilerParams(
            collective_id=0, has_side_effects=True, vmem_limit_bytes=63 << 20
        ),
    )(
        views, view_study.reshape(1, slots), pool_query, texts,
        logit_scale, logit_bias,
    )


def solution(mesh):
    in_specs = (P("dp", "mp"), P("dp"), P("mp"), P("dp", "mp"), P(), P())
    out_specs = (P("dp", "mp"), P("dp", "mp"))
    return jax.shard_map(
        on_device, mesh=mesh, in_specs=in_specs, out_specs=out_specs, check_vma=False
    )
```

time: 39.7 us -> 37.1 us (0.935)
  the two profiles are of different devices: /device:TPU:7 before, /device:TPU:1 now
where the time goes in v2:
time: 37.1 us; the launch traced here: 36.9 us
  Pallas kernels  33.1 us (89%)
  local copies, waits for them, and re-layouts  1.94 us (5%)
  between operations  1.94 us (5%)
    pallas_call x1, Pallas kernels, on_device(): pl.pallas_call(kernel, out_shape=(out, out), in_specs=[hbm, hbm, hbm, hbm...  33.1 us
    unnamed x4, local copies, waits for them, and re-layouts  1.94 us

profile of v2, /device:TPU:1, one launch (start us, length us, event | category | flops | bytes accessed | tf_op | source)
XLA Modules:
  0.0 36.9 jit_solution(4498633644370776203)
XLA Ops:
  1.9 33.1 %shard_map.77 = (bf16[16,512]{1,0:T(8,128)(2,1)}, bf16[16,512]{1,0:T(8,128)(2,1)}) custom-call(bf16[128,512]{1,0:T(8,128)(2,1)} %views_in.1, s32[1,128]{1,0:T(1,128)} %bitcast.1, bf16[512]{0:T(512)(128)(2,1)} %query_in.1, bf16[16,512]{1,0:T(8,128)(2,1)} %texts_in.1, f32[1]{0:T(128)S(6)} %copy.10.scale, f32[1]{0:T(128)S(6)} %copy.11.bias), custom_call_target="tpu_custom_call" | custom-call | tf_op jit(solution)/shard_map/pallas_call | solution.py:209
  35.0 0.0 copy-start
  35.0 1.3 %copy.12 = bf16[16,512]{1,0:T(8,128)(2,1)} copy(bf16[16,512]{1,0:T(8,128)(2,1)} %get-tuple-element.4) | data formatting | bytes 32768
  36.3 0.0 copy-done
  36.3 0.6 %copy.13 = bf16[16,512]{1,0:T(8,128)(2,1)} copy(bf16[16,512]{1,0:T(8,128)(2,1)S(1)} %copy-done) | data formatting | bytes 32768
Async XLA Ops:
  35.0 1.3 %copy-start = (bf16[16,512]{1,0:T(8,128)(2,1)S(1)}, bf16[16,512]{1,0:T(8,128)(2,1)}, u32[]{:S(2)}) copy-start(bf16[16,512]{1,0:T(8,128)(2,1)} %get-tuple-element.5) | copy-start | bytes 49156

commit v3 on v2

--- a/solution.py
+++ b/solution.py
@@ -15,7 +15,7 @@
 COL = LANES * OWN
 BLK = 8
 REP = BLK * OWN
-CHUNK = 48
+CHUNK = 32
 WIDE = WIDTH + 128
 
 NEAR = {0: 0, 1: 1, 2: 2, 3: 1}
@@ -34,8 +34,8 @@
 
 def kernel(
     views_in, study_in, query_in, texts_in, scale, bias, out_pooled, out_text,
-    views, study, query, texts, send_v, land_v, send_s, land_s, land_x, part, land_sib, col_sum, land_sum,
-    text_part, pooled_part, land_t, land_p, ssem, rsem, lsem,
+    views, study, query, texts, send_v, land_v, send_s, land_s, land_r, land_x, part, land_sib, col_sum, land_sum,
+    land_den, text_part, pooled_part, land_t, land_p, ssem, rsem, lsem,
 ):
     dp, half = lax.axis_index("dp"), lax.axis_index("mp")
     pos, lane = dp // LANES, lax.rem(dp, LANES)
@@ -52,9 +52,10 @@
     def greet(p, l, h):
         pl.semaphore_signal(barrier, inc=1, device_id=(p * LANES + l, h), device_id_type=MESH)
 
+    for dy, dx in STEPS:
+        greet(at(dy, dx), lane, other)
     for dy, dx in STEPS[:-1]:
         greet(at(dy, dx), lane, half)
-    greet(pos, lane, other)
     for k in range(1, LANES):
         for h in (other, half):
             greet(pos, lax.rem(lane + k, LANES), h)
@@ -84,14 +85,17 @@
     packed = jnp.dot(pick, views[...], preferred_element_type=F32)
     marks = jnp.broadcast_to(((ids & (COL - 1)) + 1).astype(F32), (slots, slots)).astype(BF)
     mark = nt(pick, marks)
-    parts = [packed[:, q * 128 : (q + 1) * 128] for q in range(4)] + [mark, mark]
+    ask = jnp.broadcast_to(query[...].reshape(1, WIDTH).astype(F32), (slots, WIDTH)).astype(BF)
+    score = nt(packed.astype(BF), ask)
+    place = colm == pos * SLOTS + (row & (SLOTS - 1))
+    for k, x in enumerate((score, mark)):
+        send_s[:, k, :] = jnp.sum(jnp.where(place, x, 0.0).reshape(POS, SLOTS, 128), axis=1)
+    parts = [packed[:, q * 128 : (q + 1) * 128] for q in range(4)]
     chunks = jnp.concatenate([x.reshape(POS, 1, SLOTS, 128) for x in parts], axis=1)
     send_v[...] = chunks.reshape(POS * CHUNK, 128).astype(BF)
     mine_rows = pl.ds(pl.multiple_of(pos * CHUNK, CHUNK), CHUNK)
     land_v[mine_rows] = send_v[mine_rows]
-    ask = jnp.broadcast_to(query[...].reshape(1, WIDTH).astype(F32), (SLOTS, WIDTH)).astype(BF)
-
-    pl.semaphore_wait(barrier, POS - 1 + 7)
+    pl.semaphore_wait(barrier, 2 * POS - 1 + 6)
 
     def copy(src, dst, i, p, l, h):
         return pltpu.make_async_remote_copy(
@@ -102,6 +106,10 @@
     def done(ref, sem):
         pltpu.make_async_copy(ref, ref, sem).wait()
 
+    sel = lax.rem(pos + core, 2)
+    giver = sel == half
+    copy(texts, land_r.at[half], 8, pos, cross, sel).start()
+    drains.append(lambda: done(texts, ssem.at[8]))
     for dy, dx in STEPS[:-1]:
         p = at(dy, dx)
         copy(
@@ -109,27 +117,36 @@
             land_v.at[mine_rows], 0, p, lane, half,
         ).start()
     drains.append(lambda: done(send_v.at[pl.ds(0, (POS - 1) * CHUNK)], ssem.at[0]))
+    for dy, dx in STEPS:
+        p = at(dy, dx)
+        copy(send_s.at[p], land_s.at[pos], 1, p, lane, other).start()
+    drains.append(lambda: done(send_s, ssem.at[1]))
 
     done(land_v.at[pl.ds(0, (POS - 1) * CHUNK)], rsem.at[0])
     got = land_v[...].astype(F32).reshape(POS, CHUNK // SLOTS, SLOTS, 128)
-    got = [got[:, q].reshape(slots, 128).astype(BF) for q in range(5)]
-    held = jnp.concatenate(got[:4], axis=1)
-    score = nt(ask, held)
-    send_s[...] = score
-    swap = copy(send_s, land_s, 1, pos, lane, other)
-    swap.start()
-    drains.append(swap.wait_send)
-
-    text_rows = pl.ds(pl.multiple_of((pos // 2) * OWN, OWN), OWN)
-    sel = lax.rem(pos, 2)
-    for dy, dx in STEPS:
-        copy(texts, land_x.at[half, text_rows], 2, at(dy, dx), cross, sel).start()
-    drains.append(lambda: done(land_x, ssem.at[2]))
-
-    mark_row = nt(jnp.where(colm[:SLOTS] == 0, 1.0, 0.0).astype(BF), got[4])[:1]
-    swap.wait_recv()
-    weight = jax.nn.sigmoid(score + land_s[...]).astype(BF).astype(F32)[:1]
-    table = jnp.where(mark_row == (row[:COL] + 1).astype(F32), weight, 0.0).astype(BF)
+    held = jnp.concatenate([got[:, q].reshape(slots, 128).astype(BF) for q in range(4)], axis=1)
+    score = nt(ask[:SLOTS], held)[:1]
+
+
+    @pl.when(giver)
+    def _():
+        done(land_r, rsem.at[8])
+        for dy, dx in STEPS[:-1]:
+            copy(land_r, land_x.at[pos // 2], 2, at(dy, dx), lane, half).start()
+        land_x[pos // 2] = land_r[...]
+
+    def handed():
+        @pl.when(giver)
+        def _():
+            done(land_x, ssem.at[2])
+            done(land_x.at[pl.ds(0, BLK - 1)], ssem.at[2])
+
+    drains.append(handed)
+
+    done(land_s, rsem.at[1])
+    more = jnp.sum(land_s[...], axis=0)
+    weight = jax.nn.sigmoid(score + more[:1]).astype(BF).astype(F32)
+    table = jnp.where(more[1:] == (row[:COL] + 1).astype(F32), weight, 0.0).astype(BF)
     wide = jnp.concatenate([held, jnp.ones((slots, 128), BF)], axis=1)
     sums = jnp.dot(table, wide, preferred_element_type=F32)
     part[...] = sums.astype(BF)
@@ -141,21 +158,34 @@
     z = half * 2 + zlo
     for k in (2, 1, 3):
         there = lax.rem(z + k, 4)
-        copy(col_sum, land_sum.at[z], 4, pos, lax.rem(there, 2) * 2 + core, there // 2).start()
-    land_sum[z] = col_sum[...]
+        copy(
+            col_sum.at[:, pl.ds(0, WIDTH)], land_sum.at[z], 4, pos, lax.rem(there, 2) * 2 + core, there // 2
+        ).start()
+    copy(col_sum.at[:, pl.ds(WIDTH, 128)], land_den, 7, pos, cross, half).start()
+    land_sum[z] = col_sum[:, :WIDTH]
     drains.append(lambda: done(land_sum.at[pl.ds(0, 3)], ssem.at[4]))
-
-    done(land_x, rsem.at[2])
-    raw = [land_x[0].astype(F32), land_x[1].astype(F32)]
+    drains.append(lambda: done(land_den, ssem.at[7]))
+
+    @pl.when(giver)
+    def _():
+        done(land_x.at[pl.ds(0, BLK - 1)], rsem.at[2])
+
+    @pl.when(jnp.logical_not(giver))
+    def _():
+        done(land_x, rsem.at[2])
+
+    raw = [land_x[:, h].reshape(REP, WIDTH).astype(F32) for h in range(HALVES)]
     norm = jnp.sum(raw[0] * raw[0] + raw[1] * raw[1], axis=1, keepdims=True)
     inv = lax.rsqrt(norm + 1e-06)
     report = jnp.concatenate([(x * inv).astype(BF) for x in raw], axis=1)
 
+    done(land_den, rsem.at[7])
     done(land_sum.at[pl.ds(0, 3)], rsem.at[4])
     both = [
         land_sum[2 * h].astype(F32) + land_sum[2 * h + 1].astype(F32) for h in range(HALVES)
     ]
-    mean = [x[:, :WIDTH] / x[:, WIDTH : WIDTH + 1] for x in both]
+    weights = col_sum[:, WIDTH:].astype(F32) + land_den[...].astype(F32)
+    mean = [x / weights[:, :1] for x in both]
     norm = jnp.sum(mean[0] * mean[0] + mean[1] * mean[1], axis=1, keepdims=True)
     inv = lax.rsqrt(norm + 1e-06)
     unit = jnp.concatenate([(x * inv).astype(BF) for x in mean], axis=1)
@@ -164,14 +194,14 @@
     i = lax.broadcasted_iota(jnp.int32, (COL, REP), 0)
     j = lax.broadcasted_iota(jnp.int32, (COL, REP), 1)
     study_id = pos * COL + i
-    report_id = ((2 * (j // OWN) + half) * LANES + cross) * OWN + lax.rem(j, OWN)
+    report_id = ((2 * (j // OWN) + lax.rem(half + core, 2)) * LANES + cross) * OWN + lax.rem(j, OWN)
     own = (study_id == report_id).astype(F32)
     slope = (jax.nn.sigmoid(logits) - own).astype(BF)
 
     gt = tn(slope, unit).astype(BF)
     for h in range(HALVES):
         text_part[h] = gt[:, h * WIDTH : (h + 1) * WIDTH]
-    odd = lax.rem(px + half, 2)
+    odd = lax.rem(px + half + core, 2)
     for dy in (2, 1, 3, 0):
         for dx in (2, 0):
             p = at(dy, dx + odd)
@@ -218,26 +248,28 @@
             pltpu.VMEM((OWN, WIDTH), BF),
             pltpu.VMEM((POS * CHUNK, 128), BF),
             pltpu.VMEM((POS * CHUNK, 128), BF),
-            pltpu.VMEM((SLOTS, 128), F32),
-            pltpu.VMEM((SLOTS, 128), F32),
-            pltpu.VMEM((HALVES, REP, WIDTH), BF),
+            pltpu.VMEM((POS, 2, 128), F32),
+            pltpu.VMEM((POS, 2, 128), F32),
+            pltpu.VMEM((HALVES, OWN, WIDTH), BF),
+            pltpu.VMEM((BLK, HALVES, OWN, WIDTH), BF),
             pltpu.VMEM((COL, WIDE), BF),
             pltpu.VMEM((COL, WIDE), BF),
             pltpu.VMEM((COL, WIDE), BF),
-            pltpu.VMEM((4, COL, WIDE), BF),
+            pltpu.VMEM((4, COL, WIDTH), BF),
+            pltpu.VMEM((COL, 128), BF),
             pltpu.VMEM((HALVES, REP, WIDTH), BF),
             pltpu.VMEM((HALVES, COL, WIDTH), BF),
             pltpu.VMEM((POS, OWN, WIDTH), BF),
             pltpu.VMEM((LANES * HALVES, OWN, WIDTH), BF),
-            pltpu.SemaphoreType.DMA((7,)),
-            pltpu.SemaphoreType.DMA((7,)),
+            pltpu.SemaphoreType.DMA((9,)),
+            pltpu.SemaphoreType.DMA((9,)),
             pltpu.SemaphoreType.DMA((4,)),
         ],
         compiler_params=pltpu.CompilerParams(
-            collective_id=0, has_side_effects=True, vmem_limit_bytes=63 << 20
+            collective_id=0, has_side_effects=True, vmem_limit_bytes=32 << 20
         ),
     )(
-        views, view_study.reshape(1, slots), pool_query, texts,
+        *(pltpu.with_memory_space_constraint(x, pltpu.HBM) for x in (views, view_study.reshape(1, slots), pool_query, texts)),
         logit_scale, logit_bias,
     )
 

time: 37.1 us -> 32.1 us (0.87)
  Pallas kernels: 33.1 us -> 28.8 us
  local copies, waits for them, and re-layouts: 1.94 us -> 1.21 us
    pallas_call x1, Pallas kernels: 33.1 us -> 28.8 us  [on_device(): pl.pallas_call(kernel, out_shape=(out, out), in_specs=[hbm, hbm, hbm, hbm...]
    unnamed x4 -> x2, local copies, waits for them, and re-layouts: 1.94 us -> 1.21 us
where the time goes in v3:
time: 32.1 us; the launch traced here: 32 us
  Pallas kernels  28.8 us (90%)
  between operations  1.93 us (6%)
  local copies, waits for them, and re-layouts  1.21 us (4%)
    pallas_call x1, Pallas kernels, on_device(): pl.pallas_call(kernel, out_shape=(out, out), in_specs=[hbm, hbm, hbm, hbm...  28.8 us
    unnamed x2, local copies, waits for them, and re-layouts  1.21 us

profile of v3, /device:TPU:1, one launch (start us, length us, event | category | flops | bytes accessed | tf_op | source)
XLA Modules:
  0.0 32.0 jit_solution(7451935032142183132)
XLA Ops:
  1.9 28.8 %shard_map.77 = (bf16[16,512]{1,0:T(8,128)(2,1)S(1)}, bf16[16,512]{1,0:T(8,128)(2,1)S(1)}) custom-call(bf16[128,512]{1,0:T(8,128)(2,1)} %views_in.1, s32[1,128]{1,0:T(1,128)} %bitcast.1, bf16[512]{0:T(512)(128)(2,1)} %query_in.1, bf16[16,512]{1,0:T(8,128)(2,1)} %texts_in.1, f32[1]{0:T(128)S(6)} %copy.10.scale, f32[1]{0:T(128)S(6)} %copy.11.bias), custom_call_target="tpu_custom_call" | custom-call | tf_op jit(solution)/shard_map/pallas_call | solution.py:239
  30.8 0.6 %copy.12 = bf16[16,512]{1,0:T(8,128)(2,1)} copy(bf16[16,512]{1,0:T(8,128)(2,1)S(1)} %get-tuple-element.4) | data formatting | bytes 32768
  31.4 0.6 %copy.13 = bf16[16,512]{1,0:T(8,128)(2,1)} copy(bf16[16,512]{1,0:T(8,128)(2,1)S(1)} %get-tuple-element.5) | data formatting | bytes 32768

commit v4 on v3

--- a/solution.py
+++ b/solution.py
@@ -15,7 +15,8 @@
 COL = LANES * OWN
 BLK = 8
 REP = BLK * OWN
-CHUNK = 32
+PIECE = WIDTH // 2
+CHUNK = 2 * SLOTS
 WIDE = WIDTH + 128
 
 NEAR = {0: 0, 1: 1, 2: 2, 3: 1}
@@ -47,19 +48,6 @@
     def at(dy, dx):
         return lax.rem(py + dy, SIDE) * SIDE + lax.rem(px + dx, SIDE)
 
-    barrier = pltpu.get_barrier_semaphore()
-
-    def greet(p, l, h):
-        pl.semaphore_signal(barrier, inc=1, device_id=(p * LANES + l, h), device_id_type=MESH)
-
-    for dy, dx in STEPS:
-        greet(at(dy, dx), lane, other)
-    for dy, dx in STEPS[:-1]:
-        greet(at(dy, dx), lane, half)
-    for k in range(1, LANES):
-        for h in (other, half):
-            greet(pos, lax.rem(lane + k, LANES), h)
-
     loads = [
         pltpu.make_async_copy(a, b, lsem.at[i])
         for i, (a, b) in enumerate(
@@ -68,11 +56,22 @@
     ]
     for load in loads:
         load.start()
+    barrier = pltpu.get_barrier_semaphore()
+
+    def greet(p, l, h):
+        pl.semaphore_signal(barrier, inc=1, device_id=(p * LANES + l, h), device_id_type=MESH)
+
+    for dy, dx in STEPS:
+        greet(at(dy, dx), lane, other)
+    for dy, dx in STEPS[:-1]:
+        greet(at(dy, dx), lane, half)
+    for k in range(1, LANES):
+        for h in (other, half):
+            greet(pos, lax.rem(lane + k, LANES), h)
+
     drains = []
 
-    for load in loads:
-        load.wait()
-
+    loads[0].wait()
     slots = views.shape[0]
     row = lax.broadcasted_iota(jnp.int32, (slots, slots), 0)
     colm = lax.broadcasted_iota(jnp.int32, (slots, slots), 1)
@@ -81,18 +80,26 @@
     before = (row < colm).astype(F32).astype(BF)
     hot = mine.astype(F32).astype(BF)
     rank = jnp.dot(hot, before, preferred_element_type=F32)
-    pick = jnp.where(mine & (rank == (row & 1).astype(F32)), 1.0, 0.0).astype(BF)
+    chosen = mine & (rank == (row & 1).astype(F32))
+    pick = chosen.astype(F32).astype(BF)
+    loads[1].wait()
     packed = jnp.dot(pick, views[...], preferred_element_type=F32)
-    marks = jnp.broadcast_to(((ids & (COL - 1)) + 1).astype(F32), (slots, slots)).astype(BF)
-    mark = nt(pick, marks)
-    ask = jnp.broadcast_to(query[...].reshape(1, WIDTH).astype(F32), (slots, WIDTH)).astype(BF)
-    score = nt(packed.astype(BF), ask)
-    place = colm == pos * SLOTS + (row & (SLOTS - 1))
+    loads[2].wait()
+    asked = query[...].reshape(1, WIDTH).astype(F32)
+    score = nt(jnp.broadcast_to(asked, (SLOTS, WIDTH)).astype(BF), views[...])[:1]
+    mark = ((ids & (COL - 1)) + 1).astype(F32)
+    wide_row = lax.broadcasted_iota(jnp.int32, (slots, POS * CHUNK), 0)
+    wide_col = lax.broadcasted_iota(jnp.int32, (slots, POS * CHUNK), 1)
+    place = (colm // CHUNK == lax.rem(pos, 8)) & ((colm & (SLOTS - 1)) == (row & (SLOTS - 1)))
     for k, x in enumerate((score, mark)):
+        x = jnp.sum(jnp.where(chosen, x, 0.0), axis=1, keepdims=True)
         send_s[:, k, :] = jnp.sum(jnp.where(place, x, 0.0).reshape(POS, SLOTS, 128), axis=1)
-    parts = [packed[:, q * 128 : (q + 1) * 128] for q in range(4)]
-    chunks = jnp.concatenate([x.reshape(POS, 1, SLOTS, 128) for x in parts], axis=1)
-    send_v[...] = chunks.reshape(POS * CHUNK, 128).astype(BF)
+    parts = [packed[:, q * PIECE : (q + 1) * PIECE] for q in range(2)]
+    ask = jnp.concatenate(
+        [jnp.broadcast_to(asked[:, q * PIECE : (q + 1) * PIECE], (SLOTS, PIECE)) for q in range(2)], axis=0
+    ).astype(BF)
+    chunks = jnp.concatenate([x.reshape(POS, 1, SLOTS, PIECE) for x in parts], axis=1)
+    send_v[...] = chunks.reshape(POS * CHUNK, PIECE).astype(BF)
     mine_rows = pl.ds(pl.multiple_of(pos * CHUNK, CHUNK), CHUNK)
     land_v[mine_rows] = send_v[mine_rows]
     pl.semaphore_wait(barrier, 2 * POS - 1 + 6)
@@ -108,8 +115,12 @@
 
     sel = lax.rem(pos + core, 2)
     giver = sel == half
+    loads[3].wait()
     copy(texts, land_r.at[half], 8, pos, cross, sel).start()
     drains.append(lambda: done(texts, ssem.at[8]))
+    for dy, dx in STEPS:
+        p = at(dy, dx)
+        copy(send_s.at[p], land_s.at[pos], 1, p, lane, other).start()
     for dy, dx in STEPS[:-1]:
         p = at(dy, dx)
         copy(
@@ -117,16 +128,14 @@
             land_v.at[mine_rows], 0, p, lane, half,
         ).start()
     drains.append(lambda: done(send_v.at[pl.ds(0, (POS - 1) * CHUNK)], ssem.at[0]))
-    for dy, dx in STEPS:
-        p = at(dy, dx)
-        copy(send_s.at[p], land_s.at[pos], 1, p, lane, other).start()
     drains.append(lambda: done(send_s, ssem.at[1]))
 
     done(land_v.at[pl.ds(0, (POS - 1) * CHUNK)], rsem.at[0])
-    got = land_v[...].astype(F32).reshape(POS, CHUNK // SLOTS, SLOTS, 128)
-    held = jnp.concatenate([got[:, q].reshape(slots, 128).astype(BF) for q in range(4)], axis=1)
-    score = nt(ask[:SLOTS], held)[:1]
-
+    held = land_v[...]
+    second = (lax.broadcasted_iota(jnp.int32, (1, POS * CHUNK), 1) & SLOTS) != 0
+    piece = nt(ask, held)
+    piece = jnp.where(second, piece[SLOTS : SLOTS + 1], piece[:1])
+    rest = jnp.where(second, pltpu.roll(piece, SLOTS, 1), pltpu.roll(piece, POS * CHUNK - SLOTS, 1))
 
     @pl.when(giver)
     def _():
@@ -144,11 +153,15 @@
     drains.append(handed)
 
     done(land_s, rsem.at[1])
-    more = jnp.sum(land_s[...], axis=0)
-    weight = jax.nn.sigmoid(score + more[:1]).astype(BF).astype(F32)
-    table = jnp.where(more[1:] == (row[:COL] + 1).astype(F32), weight, 0.0).astype(BF)
-    wide = jnp.concatenate([held, jnp.ones((slots, 128), BF)], axis=1)
-    sums = jnp.dot(table, wide, preferred_element_type=F32)
+    more = jnp.sum(land_s[...].reshape(2, 8, 2, 128), axis=1)
+    more = jnp.concatenate([more[0], more[1]], axis=1)
+    weight = jax.nn.sigmoid(piece + rest + more[:1]).astype(BF).astype(F32)
+    study_row = (wide_row & (COL - 1)) + 1
+    fits = (more[1:] == study_row.astype(F32)) & (((wide_row & COL) != 0) == ((wide_col & SLOTS) != 0))
+    table = jnp.where(fits, weight, 0.0).astype(BF)
+    sums = jnp.dot(table, held, preferred_element_type=F32)
+    total = jnp.dot(table[:COL], jnp.ones((POS * CHUNK, 128), BF), preferred_element_type=F32)
+    sums = jnp.concatenate([sums[:COL], sums[COL:], total], axis=1)
     part[...] = sums.astype(BF)
     sib = copy(part, land_sib, 3, pos, lane + 1 - 2 * core, half)
     sib.start()
@@ -190,27 +203,25 @@
     inv = lax.rsqrt(norm + 1e-06)
     unit = jnp.concatenate([(x * inv).astype(BF) for x in mean], axis=1)
 
-    logits = scale[0] * nt(unit, report) + bias[0]
-    i = lax.broadcasted_iota(jnp.int32, (COL, REP), 0)
-    j = lax.broadcasted_iota(jnp.int32, (COL, REP), 1)
+    logits = scale[0] * nt(report, unit) + bias[0]
+    i = lax.broadcasted_iota(jnp.int32, (REP, COL), 1)
+    j = lax.broadcasted_iota(jnp.int32, (REP, COL), 0)
     study_id = pos * COL + i
     report_id = ((2 * (j // OWN) + lax.rem(half + core, 2)) * LANES + cross) * OWN + lax.rem(j, OWN)
     own = (study_id == report_id).astype(F32)
     slope = (jax.nn.sigmoid(logits) - own).astype(BF)
 
-    gt = tn(slope, unit).astype(BF)
+    odd = lax.rem(px + half + core, 2)
     for h in range(HALVES):
-        text_part[h] = gt[:, h * WIDTH : (h + 1) * WIDTH]
-    odd = lax.rem(px + half + core, 2)
-    for dy in (2, 1, 3, 0):
-        for dx in (2, 0):
-            p = at(dy, dx + odd)
-            rows = pl.ds(pl.multiple_of((p // 2) * OWN, OWN), OWN)
-            for h in range(HALVES):
+        text_part[h] = jnp.dot(slope, unit[:, h * WIDTH : (h + 1) * WIDTH], preferred_element_type=F32).astype(BF)
+        for dy in (2, 1, 3, 0):
+            for dx in (2, 0):
+                p = at(dy, dx + odd)
+                rows = pl.ds(pl.multiple_of((p // 2) * OWN, OWN), OWN)
                 copy(text_part.at[h, rows], land_t.at[pos], 5, p, cross, h).start()
     drains.append(lambda: done(land_t, ssem.at[5]))
 
-    gp = jnp.dot(slope, report, preferred_element_type=F32).astype(BF)
+    gp = tn(slope, report).astype(BF)
     for h in range(HALVES):
         pooled_part[h] = gp[:, h * WIDTH : (h + 1) * WIDTH]
     me = lane * 2 + half
@@ -223,9 +234,11 @@
     drains.append(lambda: done(land_p.at[pl.ds(0, 7)], ssem.at[6]))
 
     done(land_p.at[pl.ds(0, 7)], rsem.at[6])
-    out_pooled[...] = jnp.sum(land_p[...].astype(F32), axis=0).astype(BF)
+    out_pooled[1] = jnp.zeros((OWN, WIDTH), BF)
+    out_text[1] = jnp.zeros((OWN, WIDTH), BF)
+    out_pooled[0] = jnp.sum(land_p[...].astype(F32), axis=0).astype(BF)
     done(land_t, rsem.at[5])
-    out_text[...] = jnp.sum(land_t[...].astype(F32), axis=0).astype(BF)
+    out_text[0] = jnp.sum(land_t[...].astype(F32), axis=0).astype(BF)
     for drain in drains:
         drain()
 
@@ -235,8 +248,8 @@
     vmem = pl.BlockSpec(memory_space=pltpu.VMEM)
     hbm = pl.BlockSpec(memory_space=pltpu.HBM)
     smem = pl.BlockSpec(memory_space=pltpu.SMEM)
-    out = jax.ShapeDtypeStruct((OWN, WIDTH), BF)
-    return pl.pallas_call(
+    out = jax.ShapeDtypeStruct((2, OWN, WIDTH), BF)
+    res = pl.pallas_call(
         kernel,
         out_shape=(out, out),
         in_specs=[hbm, hbm, hbm, hbm, smem, smem],
@@ -246,8 +259,8 @@
             pltpu.VMEM((1, slots), jnp.int32),
             pltpu.VMEM((WIDTH,), BF),
             pltpu.VMEM((OWN, WIDTH), BF),
-            pltpu.VMEM((POS * CHUNK, 128), BF),
-            pltpu.VMEM((POS * CHUNK, 128), BF),
+            pltpu.VMEM((POS * CHUNK, PIECE), BF),
+            pltpu.VMEM((POS * CHUNK, PIECE), BF),
             pltpu.VMEM((POS, 2, 128), F32),
             pltpu.VMEM((POS, 2, 128), F32),
             pltpu.VMEM((HALVES, OWN, WIDTH), BF),
@@ -272,6 +285,10 @@
         *(pltpu.with_memory_space_constraint(x, pltpu.HBM) for x in (views, view_study.reshape(1, slots), pool_query, texts)),
         logit_scale, logit_bias,
     )
+    zero = jnp.zeros((), BF)
+    return tuple(
+        lax.reduce(tuple(res), (zero, zero), lambda a, b: (a[0] + b[0], a[1] + b[1]), (0,))
+    )
 
 
 def solution(mesh):

time: 32.1 us -> 30.5 us (0.950)
  local copies, waits for them, and re-layouts: 1.21 us -> 0 us
  Pallas kernels: 28.8 us -> 27.8 us
  other arithmetic: 0 us -> 0.65 us
    unnamed x2 -> x0, local copies, waits for them, and re-layouts: 1.21 us -> none
    pallas_call x1, Pallas kernels: 28.8 us -> 27.8 us  [on_device(): pl.pallas_call(kernel, out_shape=(out, out), in_specs=[hbm, hbm, hbm, hbm...]
    another operation x0 -> x1, other arithmetic: none -> 0.65 us  [on_device(): lax.reduce(tuple(res), (zero, zero), lambda a, b: (a[0] + b[0], a[1] + b[...]
where the time goes in v4:
time: 30.5 us; the launch traced here: 30.4 us
  Pallas kernels  27.8 us (91%)
  between operations  1.93 us (6%)
  other arithmetic  0.65 us (2%)
    pallas_call x1, Pallas kernels, on_device(): pl.pallas_call(kernel, out_shape=(out, out), in_specs=[hbm, hbm, hbm, hbm...  27.8 us
    another operation x1, other arithmetic, on_device(): lax.reduce(tuple(res), (zero, zero), lambda a, b: (a[0] + b[0], a[1] + b[...  0.65 us

profile of v4, /device:TPU:1, one launch (start us, length us, event | category | flops | bytes accessed | tf_op | source)
XLA Modules:
  0.0 30.4 jit_solution(6740494561739862387)
XLA Ops:
  1.9 27.8 %shard_map.77 = (bf16[2,16,512]{2,1,0:T(8,128)(2,1)S(1)}, bf16[2,16,512]{2,1,0:T(8,128)(2,1)S(1)}) custom-call(bf16[128,512]{1,0:T(8,128)(2,1)} %views_in.1, s32[1,128]{1,0:T(1,128)} %bitcast.1, bf16[512]{0:T(512)(128)(2,1)} %query_in.1, bf16[16,512]{1,0:T(8,128)(2,1)} %texts_in.1, f32[1]{0:T(128)S(6)} %copy.8.scale, f32[1]{0:T(128)S(6)} %copy.9.bias), custom_call_target="tpu_custom_call" | custom-call | tf_op jit(solution)/shard_map/pallas_call | solution.py:252
  29.7 0.7 %reduce.15 = (bf16[16,512]{1,0:T(8,128)(2,1)}, bf16[16,512]{1,0:T(8,128)(2,1)}) reduce(bf16[2,16,512]{2,1,0:T(8,128)(2,1)S(1)} %get-tuple-element.4, bf16[2,16,512]{2,1,0:T(8,128)(2,1)S(1)} %get-tuple-element.5, bf16[]{:T(256)} %constant.0.clone.1, bf16[]{:T(256)} %constant.0.clone.1), dimensions={0}, to_apply=%region_0.0 | reduce | flops 16384 | bytes 98308 | tf_op jit(solution)/shard_map/reduce | solution.py:290

commit v5 on v4

--- a/solution.py
+++ b/solution.py
@@ -8,7 +8,7 @@
 MESH = pl.DeviceIdType.MESH
 BF, F32 = jnp.bfloat16, jnp.float32
 SIDE = 4
-POS, LANES, HALVES = 16, 4, 2
+POS, LANES, HALVES, CORES = 16, 4, 2, 2
 OWN = 16
 WIDTH = 512
 SLOTS = 8
@@ -36,17 +36,20 @@
 def kernel(
     views_in, study_in, query_in, texts_in, scale, bias, out_pooled, out_text,
     views, study, query, texts, send_v, land_v, send_s, land_s, land_r, land_x, part, land_sib, col_sum, land_sum,
-    land_den, text_part, pooled_part, land_t, land_p, ssem, rsem, lsem,
+    land_den, text_part, pooled_part, pooled_sum, land_q, land_t, land_p, ssem, rsem, lsem,
 ):
     dp, half = lax.axis_index("dp"), lax.axis_index("mp")
-    pos, lane = dp // LANES, lax.rem(dp, LANES)
-    py, px = pos // SIDE, lax.rem(pos, SIDE)
-    zlo, core = lane // 2, lax.rem(lane, 2)
+    pos, lane = lax.div(dp, LANES), lax.rem(dp, LANES)
+    py, px = lax.div(pos, SIDE), lax.rem(pos, SIDE)
+    zlo, core = lax.div(lane, 2), lax.rem(lane, 2)
     other = 1 - half
     cross = (1 - zlo) * 2 + core
 
+    rows_of = [lax.rem(py + d, SIDE) * SIDE for d in range(SIDE)]
+    columns_of = [lax.rem(px + d, SIDE) for d in range(SIDE)]
+
     def at(dy, dx):
-        return lax.rem(py + dy, SIDE) * SIDE + lax.rem(px + dx, SIDE)
+        return rows_of[dy] + columns_of[dx]
 
     loads = [
         pltpu.make_async_copy(a, b, lsem.at[i])
@@ -198,7 +201,8 @@
         land_sum[2 * h].astype(F32) + land_sum[2 * h + 1].astype(F32) for h in range(HALVES)
     ]
     weights = col_sum[:, WIDTH:].astype(F32) + land_den[...].astype(F32)
-    mean = [x / weights[:, :1] for x in both]
+    share = 1.0 / weights[:, :1]
+    mean = [x * share for x in both]
     norm = jnp.sum(mean[0] * mean[0] + mean[1] * mean[1], axis=1, keepdims=True)
     inv = lax.rsqrt(norm + 1e-06)
     unit = jnp.concatenate([(x * inv).astype(BF) for x in mean], axis=1)
@@ -212,28 +216,31 @@
     slope = (jax.nn.sigmoid(logits) - own).astype(BF)
 
     odd = lax.rem(px + half + core, 2)
+    odd_column = lax.rem(half + core, 2)
+    given = [(y, lax.rem(px + dx + odd, SIDE)) for y in (rows_of[2], rows_of[1], rows_of[3], rows_of[0]) for dx in (2, 0)]
     for h in range(HALVES):
         text_part[h] = jnp.dot(slope, unit[:, h * WIDTH : (h + 1) * WIDTH], preferred_element_type=F32).astype(BF)
-        for dy in (2, 1, 3, 0):
-            for dx in (2, 0):
-                p = at(dy, dx + odd)
-                rows = pl.ds(pl.multiple_of((p // 2) * OWN, OWN), OWN)
-                copy(text_part.at[h, rows], land_t.at[pos], 5, p, cross, h).start()
+        for y, x in given:
+            rows = pl.ds(pl.multiple_of((y + x - odd_column) * BLK, OWN), OWN)
+            copy(text_part.at[h, rows], land_t.at[pos], 5, y + x, cross, h).start()
     drains.append(lambda: done(land_t, ssem.at[5]))
 
     gp = tn(slope, report).astype(BF)
     for h in range(HALVES):
-        pooled_part[h] = gp[:, h * WIDTH : (h + 1) * WIDTH]
-    me = lane * 2 + half
-    for k in range(1, 8):
-        there = lax.rem(me + k, 8)
-        l, h = there // 2, lax.rem(there, 2)
-        rows = pl.ds(pl.multiple_of(l * OWN, OWN), OWN)
-        copy(pooled_part.at[h, rows], land_p.at[me], 6, pos, l, h).start()
-    land_p[me] = pooled_part[half, pl.ds(pl.multiple_of(lane * OWN, OWN), OWN)]
-    drains.append(lambda: done(land_p.at[pl.ds(0, 7)], ssem.at[6]))
-
-    done(land_p.at[pl.ds(0, 7)], rsem.at[6])
+        pooled_part[h] = gp[:, h * WIDTH : (h + 1) * WIDTH].reshape(2, CORES, OWN, WIDTH)
+    pair = copy(pooled_part.at[:, :, 1 - core], land_q, 9, pos, lane + 1 - 2 * core, half)
+    pair.start()
+    drains.append(pair.wait_send)
+    pair.wait_recv()
+    pooled_sum[...] = (pooled_part[:, :, core].astype(F32) + land_q[...].astype(F32)).astype(BF)
+    for k in (2, 1, 3):
+        there = lax.rem(z + k, 4)
+        h, l = lax.div(there, 2), lax.rem(there, 2)
+        copy(pooled_sum.at[h, l], land_p.at[z], 6, pos, l * 2 + core, h).start()
+    land_p[z] = pooled_sum[half, zlo]
+    drains.append(lambda: done(land_p.at[pl.ds(0, 3)], ssem.at[6]))
+
+    done(land_p.at[pl.ds(0, 3)], rsem.at[6])
     out_pooled[1] = jnp.zeros((OWN, WIDTH), BF)
     out_text[1] = jnp.zeros((OWN, WIDTH), BF)
     out_pooled[0] = jnp.sum(land_p[...].astype(F32), axis=0).astype(BF)
@@ -271,11 +278,13 @@
             pltpu.VMEM((4, COL, WIDTH), BF),
             pltpu.VMEM((COL, 128), BF),
             pltpu.VMEM((HALVES, REP, WIDTH), BF),
-            pltpu.VMEM((HALVES, COL, WIDTH), BF),
+            pltpu.VMEM((HALVES, 2, CORES, OWN, WIDTH), BF),
+            pltpu.VMEM((HALVES, 2, OWN, WIDTH), BF),
+            pltpu.VMEM((HALVES, 2, OWN, WIDTH), BF),
             pltpu.VMEM((POS, OWN, WIDTH), BF),
-            pltpu.VMEM((LANES * HALVES, OWN, WIDTH), BF),
-            pltpu.SemaphoreType.DMA((9,)),
-            pltpu.SemaphoreType.DMA((9,)),
+            pltpu.VMEM((4, OWN, WIDTH), BF),
+            pltpu.SemaphoreType.DMA((10,)),
+            pltpu.SemaphoreType.DMA((10,)),
             pltpu.SemaphoreType.DMA((4,)),
         ],
         compiler_params=pltpu.CompilerParams(

time: 30.5 us -> 30.3 us (level)
  no operation moved by 1% of the time
where the time goes in v5:
time: 30.3 us; the launch traced here: 30.2 us
  Pallas kernels  27.6 us (91%)
  between operations  1.93 us (6%)
  other arithmetic  0.65 us (2%)
    pallas_call x1, Pallas kernels, on_device(): pl.pallas_call(kernel, out_shape=(out, out), in_specs=[hbm, hbm, hbm, hbm...  27.6 us
    another operation x1, other arithmetic, on_device(): lax.reduce(tuple(res), (zero, zero), lambda a, b: (a[0] + b[0], a[1] + b[...  0.65 us

profile of v5, /device:TPU:1, one launch (start us, length us, event | category | flops | bytes accessed | tf_op | source)
XLA Modules:
  0.0 30.2 jit_solution(12268178586351334475)
XLA Ops:
  1.9 27.6 %shard_map.77 = (bf16[2,16,512]{2,1,0:T(8,128)(2,1)S(1)}, bf16[2,16,512]{2,1,0:T(8,128)(2,1)S(1)}) custom-call(bf16[128,512]{1,0:T(8,128)(2,1)} %views_in.1, s32[1,128]{1,0:T(1,128)} %bitcast.1, bf16[512]{0:T(512)(128)(2,1)} %query_in.1, bf16[16,512]{1,0:T(8,128)(2,1)} %texts_in.1, f32[1]{0:T(128)S(6)} %copy.8.scale, f32[1]{0:T(128)S(6)} %copy.9.bias), custom_call_target="tpu_custom_call" | custom-call | tf_op jit(solution)/shard_map/pallas_call | solution.py:259
  29.5 0.7 %reduce.15 = (bf16[16,512]{1,0:T(8,128)(2,1)}, bf16[16,512]{1,0:T(8,128)(2,1)}) reduce(bf16[2,16,512]{2,1,0:T(8,128)(2,1)S(1)} %get-tuple-element.4, bf16[2,16,512]{2,1,0:T(8,128)(2,1)S(1)} %get-tuple-element.5, bf16[]{:T(256)} %constant.0.clone.1, bf16[]{:T(256)} %constant.0.clone.1), dimensions={0}, to_apply=%region_0.0 | reduce | flops 16384 | bytes 98308 | tf_op jit(solution)/shard_map/reduce | solution.py:299

commit v6 on v5

--- a/solution.py
+++ b/solution.py
@@ -133,6 +133,21 @@
     drains.append(lambda: done(send_v.at[pl.ds(0, (POS - 1) * CHUNK)], ssem.at[0]))
     drains.append(lambda: done(send_s, ssem.at[1]))
 
+    @pl.when(giver)
+    def _():
+        done(land_r, rsem.at[8])
+        for dy, dx in STEPS[:8]:
+            copy(land_r, land_x.at[pos // 2], 2, at(dy, dx), lane, half).start()
+        land_x[pos // 2] = land_r[...]
+
+    def handed():
+        @pl.when(giver)
+        def _():
+            done(land_x, ssem.at[2])
+            done(land_x.at[pl.ds(0, BLK - 1)], ssem.at[2])
+
+    drains.append(handed)
+
     done(land_v.at[pl.ds(0, (POS - 1) * CHUNK)], rsem.at[0])
     held = land_v[...]
     second = (lax.broadcasted_iota(jnp.int32, (1, POS * CHUNK), 1) & SLOTS) != 0
@@ -142,18 +157,8 @@
 
     @pl.when(giver)
     def _():
-        done(land_r, rsem.at[8])
-        for dy, dx in STEPS[:-1]:
+        for dy, dx in STEPS[8:-1]:
             copy(land_r, land_x.at[pos // 2], 2, at(dy, dx), lane, half).start()
-        land_x[pos // 2] = land_r[...]
-
-    def handed():
-        @pl.when(giver)
-        def _():
-            done(land_x, ssem.at[2])
-            done(land_x.at[pl.ds(0, BLK - 1)], ssem.at[2])
-
-    drains.append(handed)
 
     done(land_s, rsem.at[1])
     more = jnp.sum(land_s[...].reshape(2, 8, 2, 128), axis=1)
@@ -218,7 +223,7 @@
     odd = lax.rem(px + half + core, 2)
     odd_column = lax.rem(half + core, 2)
     given = [(y, lax.rem(px + dx + odd, SIDE)) for y in (rows_of[2], rows_of[1], rows_of[3], rows_of[0]) for dx in (2, 0)]
-    for h in range(HALVES):
+    for h in (0,):
         text_part[h] = jnp.dot(slope, unit[:, h * WIDTH : (h + 1) * WIDTH], preferred_element_type=F32).astype(BF)
         for y, x in given:
             rows = pl.ds(pl.multiple_of((y + x - odd_column) * BLK, OWN), OWN)
@@ -230,6 +235,11 @@
         pooled_part[h] = gp[:, h * WIDTH : (h + 1) * WIDTH].reshape(2, CORES, OWN, WIDTH)
     pair = copy(pooled_part.at[:, :, 1 - core], land_q, 9, pos, lane + 1 - 2 * core, half)
     pair.start()
+    for h in (1,):
+        text_part[h] = jnp.dot(slope, unit[:, h * WIDTH : (h + 1) * WIDTH], preferred_element_type=F32).astype(BF)
+        for y, x in given:
+            rows = pl.ds(pl.multiple_of((y + x - odd_column) * BLK, OWN), OWN)
+            copy(text_part.at[h, rows], land_t.at[pos], 5, y + x, cross, h).start()
     drains.append(pair.wait_send)
     pair.wait_recv()
     pooled_sum[...] = (pooled_part[:, :, core].astype(F32) + land_q[...].astype(F32)).astype(BF)

time: 30.3 us -> 30.3 us (level)
  no operation moved by 1% of the time
where the time goes in v6:
time: 30.3 us; the launch traced here: 30.1 us
  Pallas kernels  27.6 us (91%)
  between operations  1.93 us (6%)
  other arithmetic  0.65 us (2%)
    pallas_call x1, Pallas kernels, on_device(): pl.pallas_call(kernel, out_shape=(out, out), in_specs=[hbm, hbm, hbm, hbm...  27.6 us
    another operation x1, other arithmetic, on_device(): lax.reduce(tuple(res), (zero, zero), lambda a, b: (a[0] + b[0], a[1] + b[...  0.65 us

profile of v6, /device:TPU:1, one launch (start us, length us, event | category | flops | bytes accessed | tf_op | source)
XLA Modules:
  0.0 30.1 jit_solution(4837375169679065241)
XLA Ops:
  1.9 27.6 %shard_map.77 = (bf16[2,16,512]{2,1,0:T(8,128)(2,1)S(1)}, bf16[2,16,512]{2,1,0:T(8,128)(2,1)S(1)}) custom-call(bf16[128,512]{1,0:T(8,128)(2,1)} %views_in.1, s32[1,128]{1,0:T(1,128)} %bitcast.1, bf16[512]{0:T(512)(128)(2,1)} %query_in.1, bf16[16,512]{1,0:T(8,128)(2,1)} %texts_in.1, f32[1]{0:T(128)S(6)} %copy.8.scale, f32[1]{0:T(128)S(6)} %copy.9.bias), custom_call_target="tpu_custom_call" | custom-call | tf_op jit(solution)/shard_map/pallas_call | solution.py:269
  29.5 0.7 %reduce.15 = (bf16[16,512]{1,0:T(8,128)(2,1)}, bf16[16,512]{1,0:T(8,128)(2,1)}) reduce(bf16[2,16,512]{2,1,0:T(8,128)(2,1)S(1)} %get-tuple-element.4, bf16[2,16,512]{2,1,0:T(8,128)(2,1)S(1)} %get-tuple-element.5, bf16[]{:T(256)} %constant.0.clone.1, bf16[]{:T(256)} %constant.0.clone.1), dimensions={0}, to_apply=%region_0.0 | reduce | flops 16384 | bytes 98308 | tf_op jit(solution)/shard_map/reduce | solution.py:309

commit v7 on v6

--- a/solution.py
+++ b/solution.py
@@ -254,10 +254,10 @@
     out_pooled[1] = jnp.zeros((OWN, WIDTH), BF)
     out_text[1] = jnp.zeros((OWN, WIDTH), BF)
     out_pooled[0] = jnp.sum(land_p[...].astype(F32), axis=0).astype(BF)
+    for drain in drains:
+        drain()
     done(land_t, rsem.at[5])
     out_text[0] = jnp.sum(land_t[...].astype(F32), axis=0).astype(BF)
-    for drain in drains:
-        drain()
 
 
 def on_device(views, view_study, pool_query, texts, logit_scale, logit_bias):

time: 30.3 us -> 30.3 us (level)
  no operation moved by 1% of the time
where the time goes in v7:
time: 30.3 us; the launch traced here: 30.1 us
  Pallas kernels  27.6 us (91%)
  between operations  1.93 us (6%)
  other arithmetic  0.65 us (2%)
    pallas_call x1, Pallas kernels, on_device(): pl.pallas_call(kernel, out_shape=(out, out), in_specs=[hbm, hbm, hbm, hbm...  27.6 us
    another operation x1, other arithmetic, on_device(): lax.reduce(tuple(res), (zero, zero), lambda a, b: (a[0] + b[0], a[1] + b[...  0.65 us

profile of v7, /device:TPU:1, one launch (start us, length us, event | category | flops | bytes accessed | tf_op | source)
XLA Modules:
  0.0 30.1 jit_solution(6797549855970580373)
XLA Ops:
  1.9 27.6 %shard_map.77 = (bf16[2,16,512]{2,1,0:T(8,128)(2,1)S(1)}, bf16[2,16,512]{2,1,0:T(8,128)(2,1)S(1)}) custom-call(bf16[128,512]{1,0:T(8,128)(2,1)} %views_in.1, s32[1,128]{1,0:T(1,128)} %bitcast.1, bf16[512]{0:T(512)(128)(2,1)} %query_in.1, bf16[16,512]{1,0:T(8,128)(2,1)} %texts_in.1, f32[1]{0:T(128)S(6)} %copy.8.scale, f32[1]{0:T(128)S(6)} %copy.9.bias), custom_call_target="tpu_custom_call" | custom-call | tf_op jit(solution)/shard_map/pallas_call | solution.py:269
  29.5 0.7 %reduce.15 = (bf16[16,512]{1,0:T(8,128)(2,1)}, bf16[16,512]{1,0:T(8,128)(2,1)}) reduce(bf16[2,16,512]{2,1,0:T(8,128)(2,1)S(1)} %get-tuple-element.4, bf16[2,16,512]{2,1,0:T(8,128)(2,1)S(1)} %get-tuple-element.5, bf16[]{:T(256)} %constant.0.clone.1, bf16[]{:T(256)} %constant.0.clone.1), dimensions={0}, to_apply=%region_0.0 | reduce | flops 16384 | bytes 98308 | tf_op jit(solution)/shard_map/reduce | solution.py:309
